TPU v7x, 32 devices: a whole 2x2x4 slice. The times are simulated.
32 devices in a mesh: group: 2 (over y), dp: 8 (over z, x), fsdp: 2 (over core).
Axes of the slice: x: 2, y: 2, z: 4, core: 2. Of those that a mesh axis runs over, the one named last changes fastest.
Arguments:
- patches: bfloat16 [4, 3584, 1536], P(('group', 'fsdp'), 'dp'), parts along dimension 0, may hold values from -6 to 6
- ln_gain: float32 [1536], replicated, may hold values from 0.25 to 1.75
- ln_bias: float32 [1536], replicated, may hold values from -3 to 3
- qkv_weight: bfloat16 [1536, 4608], P(None, ('dp', 'fsdp')), may hold values from -0.15625 to 0.15625
- qkv_bias: float32 [4608], replicated, may hold values from -7 to 7
- lengths: int32 [4, 8, 8], P(('group', 'fsdp')), parts along dimension 0, may hold values from 14 to 56, as said below
- destinations: int32 [4, 8, 8], P(('group', 'fsdp')), parts along dimension 0, may hold values from 0 to 7, each once within a row
Outputs:
- context: bfloat16 [4, 3584, 1536], P(('group', 'fsdp'), 'dp'), parts along dimension 0
There are 2 independent parts, one for each index of `group`. A program takes and returns all parts, laid end to end along the dimension named above; an argument that names none is the same for every part. Nothing has to cross between parts.
Inputs may be any that keep to these rules, and one draw needn't show every extreme that they name: `lengths`: between 14 and 56; each device's row reaches 56. `destinations`: each device sends exactly one image to every dp index, itself included.
All inputs are finite; a program needn't handle non-finite values.
Results may differ from a plain program's by a relative error of at most 0.0024.
The roundings to bfloat16 on the way count: a program that leaves them out, or rounds other values in their place, can miss the bound.
Values may be sent and summed in bfloat16 or wider, within the bound.
A program may use at most 128 MiB of HBM per device.

v0:
```python
import jax
import jax.numpy as jnp
from jax import lax
from jax.sharding import PartitionSpec as P

HEADS = 24
HEAD = 64


def on_device(patches, ln_gain, ln_bias, qkv_weight, qkv_bias, lengths, destinations):
    n_dp = lax.axis_size("dp")
    me_dp = lax.axis_index("dp")
    rows = patches[0]
    width = rows.shape[1]
    cap = rows.shape[0] // n_dp
    table_len = lengths[0]
    table_dest = destinations[0]
    own_len = lax.dynamic_index_in_dim(table_len, me_dp, 0, keepdims=False)
    own_dest = lax.dynamic_index_in_dim(table_dest, me_dp, 0, keepdims=False)
    offsets = jnp.cumsum(own_len) - own_len
    onehot = own_dest[None, :] == jnp.arange(n_dp, dtype=jnp.int32)[:, None]
    slot_len = jnp.sum(jnp.where(onehot, own_len[None, :], 0), axis=1)
    slot_off = jnp.sum(jnp.where(onehot, offsets[None, :], 0), axis=1)
    position = jnp.arange(cap, dtype=jnp.int32)
    send_live = position[None, :] < slot_len[:, None]
    index = jnp.where(send_live, slot_off[:, None] + position[None, :], 0)
    picked = jnp.take(rows, index.reshape(-1), axis=0).reshape(n_dp, cap, width)
    outgoing = jnp.where(send_live[:, :, None], picked, jnp.zeros((), picked.dtype))
    incoming = lax.all_to_all(outgoing, "dp", split_axis=0, concat_axis=0, tiled=True)
    recv_len = jnp.sum(jnp.where(table_dest == me_dp, table_len, 0), axis=1)
    flat = incoming.reshape(n_dp * cap, width).astype(jnp.float32)
    mean = jnp.mean(flat, axis=1, keepdims=True)
    centred = flat - mean
    var = jnp.mean(centred * centred, axis=1, keepdims=True)
    normed = (centred * lax.rsqrt(var + 1e-06) * ln_gain + ln_bias).astype(jnp.bfloat16)
    qkv = (
        jnp.dot(
            normed,
            lax.all_gather(qkv_weight, ("dp", "fsdp"), axis=1, tiled=True),
            preferred_element_type=jnp.float32,
        )
        + qkv_bias
    ).astype(jnp.bfloat16)
    query = qkv[:, :width].reshape(n_dp, cap, HEADS, HEAD)
    keys = qkv[:, width : 2 * width].reshape(n_dp, cap, HEADS, HEAD)
    values = qkv[:, 2 * width :].reshape(n_dp, cap, HEADS, HEAD)
    scores = jnp.einsum(
        "sqhe,skhe->shqk", query, keys, preferred_element_type=jnp.float32
    ) * HEAD ** (-0.5)
    live = position[None, :] < recv_len[:, None]
    scores = jnp.where(live[:, None, None, :], scores, jnp.float32(-1e30))
    top = jnp.max(scores, axis=3, keepdims=True)
    expo = jnp.exp(scores - top)
    probs = (expo / jnp.sum(expo, axis=3, keepdims=True)).astype(jnp.bfloat16)
    context = jnp.einsum("shqk,skhe->sqhe", probs, values, preferred_element_type=jnp.float32)
    context = jnp.where(live[:, :, None, None], context, jnp.float32(0.0))
    return context.reshape(1, n_dp * cap, width).astype(jnp.bfloat16)


def solution(mesh):
    placed = (
        P(("group", "fsdp"), "dp", None),
        P(),
        P(),
        P(None, ("dp", "fsdp")),
        P(),
        P(("group", "fsdp"), None, None),
        P(("group", "fsdp"), None, None),
    )
    return jax.shard_map(
        on_device,
        mesh=mesh,
        in_specs=placed,
        out_specs=P(("group", "fsdp"), "dp", None),
        check_vma=False,
    )
```

profile of v0, /device:TPU:1, one launch (start us, length us, event | category | flops | bytes accessed | tf_op | source)
XLA Modules:
  0.0 204.1 jit_solution(17744358713969929402)
XLA Ops:
  6.5 0.0 copy-start
  6.5 0.0 all-gather.2.cloned.1.call-start
  6.5 0.7 all-gather.2.cloned.1.call-update
  7.3 0.7 fusion.18
  8.0 0.2 reduce-window.8
  8.1 0.7 dynamic-slice_bitcast_fusion
  8.8 0.7 bitcast_subtract_fusion.1
  9.5 0.1 select_reduce_fusion.1
  9.7 0.1 add_select_fusion
  9.7 0.1 select_n.76
  9.9 0.0 copy-done
  9.9 2.2 %gather_fusion = bf16[448,1536]{1,0:T(8,128)(2,1)S(1)} fusion(bf16[448,1536]{1,0:T(8,128)(2,1)S(1)} %bitcast.28, s32[1024]{0:T(1024)S(1)} %pad_clamp_fusion), kind=kCustom, calls=%fused_computation | custom fusion | bytes 2754304 | tf_op jit(solution)/shard_map/jit(_take)/gather | solution.py:27
  12.1 0.1 iota_compare_fusion.1
  12.2 0.0 copy-start.4
  12.2 0.0 copy-start.5
  12.2 1.3 select_select_fusion
  13.5 0.0 copy-start.2
  13.5 0.0 copy-start.3
  13.5 6.5 %all-to-all-start = ((bf16[8,56,1536]{2,1,0:T(8,128)(2,1)}), bf16[8,56,1536]{2,1,0:T(8,128)(2,1)S(1)}, u32[]{:S(2)}, u32[]{:S(2)}) async-start(bf16[8,56,1536]{2,1,0:T(8,128)(2,1)} %select_select_fusion), calls=%async_computation | async-start | bytes 2752512 | tf_op jit(solution)/shard_map/all_to_all | solution.py:29
  20.0 0.0 copy-done.4
  20.0 0.0 copy-done.5
  20.0 0.1 select_reduce_fusion.2
  20.1 0.1 iota_compare_fusion.2
  20.2 0.0 copy-start.6
  20.2 59.6 %all-to-all-done = bf16[8,56,1536]{2,1,0:T(8,128)(2,1)S(1)} async-done(((bf16[8,56,1536]{2,1,0:T(8,128)(2,1)}), bf16[8,56,1536]{2,1,0:T(8,128)(2,1)S(1)}, u32[]{:S(2)}, u32[]{:S(2)}) %all-to-all-start) | async-done | bytes 1376288 | tf_op jit(solution)/shard_map/all_to_all | solution.py:29
  79.8 0.3 convert_reduce_fusion
  80.0 0.1 div.17
  80.1 0.5 multiply_reduce_fusion
  80.6 0.1 rsqrt.12
  80.7 0.0 copy-done.2
  80.7 0.0 copy-done.3
  80.7 1.7 fusion.7
  82.4 68.9 %all-gather.2.cloned.1.call-done = bf16[1536,4608]{0,1:T(8,128)(2,1)} async-done(((bf16[1536,288]{0,1:T(8,128)(2,1)}), bf16[1536,4608]{0,1:T(8,128)(2,1)}) %all-gather.2.cloned.1.call-update) | async-done | bytes 14155792 | tf_op jit(solution)/shard_map/all_gather | solution.py:39
  151.2 0.0 copy-done.6
  151.3 15.1 %add_convert_fusion = bf16[448,4608]{1,0:T(8,128)(2,1)} fusion(bf16[448,1536]{1,0:T(8,128)(2,1)} %fusion.7, bf16[1536,4608]{0,1:T(8,128)(2,1)} %all-gather.2.cloned.1.call-done, f32[4608]{0:T(1024)S(1)} %copy-done.6), kind=kOutput, calls=%fused_computation.2 | convolution fusion | flops 6345916416 | bytes 19679232 | tf_op jit(solution)/shard_map/dot_general | solution.py:37
  166.4 4.0 %fusion.23 = (bf16[448,1536]{1,0:T(8,128)(2,1)S(1)}, bf16[448,1536]{1,0:T(8,128)(2,1)}, bf16[448,1536]{1,0:T(8,128)(2,1)}) fusion(bf16[448,4608]{1,0:T(8,128)(2,1)} %add_convert_fusion), kind=kLoop, calls=%fused_computation.46 | loop fusion | bytes 8257536 | tf_op jit(solution)/shard_map/slice | solution.py:46
  170.3 4.4 %reshape.238 = bf16[8,56,24,64]{3,2,1,0:T(8,128)(2,1)} reshape(bf16[448,1536]{1,0:T(8,128)(2,1)} %get-tuple-element.11) | data formatting | bytes 2752512 | tf_op jit(solution)/shard_map/reshape | solution.py:44
  174.8 4.4 %reshape.239 = bf16[8,56,24,64]{3,2,1,0:T(8,128)(2,1)} reshape(bf16[448,1536]{1,0:T(8,128)(2,1)} %get-tuple-element.10) | data formatting | bytes 2752512 | tf_op jit(solution)/shard_map/reshape | solution.py:45
  179.2 2.6 %reshape.237 = bf16[8,56,24,64]{3,2,1,0:T(8,128)(2,1)} reshape(bf16[448,1536]{1,0:T(8,128)(2,1)S(1)} %get-tuple-element.9) | data formatting | bytes 2752512 | tf_op jit(solution)/shard_map/reshape | solution.py:46
  181.8 4.2 %fusion.9 = f32[8,24,56,56]{2,3,1,0:T(8,128)S(1)} fusion(bf16[8,56,24,64]{3,2,1,0:T(8,128)(2,1)} %reshape.239, bf16[8,56,24,64]{3,2,1,0:T(8,128)(2,1)} %reshape.238), kind=kOutput, calls=%fused_computation.16 | convolution fusion | flops 77070336 | bytes 5160960 | tf_op jit(solution)/shard_map/sqhe,skhe->shqk/dot_general | solution.py:47
  186.0 0.0 copy-start.1
  186.0 2.7 %fusion.24 = (f32[8,24,56]{2,1,0:T(8,128)S(1)}, f32[8,24,56,56]{2,3,1,0:T(8,128)S(1)}) fusion(f32[8,24,56,56]{2,3,1,0:T(8,128)S(1)} %fusion.9, pred[8,56]{1,0:T(8,128)(4,1)S(1)} %iota_compare_fusion.2), kind=kOutput, calls=%fused_computation.47 | output fusion | flops 3612727 | bytes 4860352 | tf_op jit(solution)/shard_map/sub | solution.py:53
  188.7 0.0 copy-done.1
  188.7 2.0 fusion.3
  190.7 2.0 copy.21
  192.7 4.6 %convert_element_type.44 = bf16[1,448,1536]{2,1,0:T(8,128)(2,1)} reshape(bf16[8,56,24,64]{3,2,1,0:T(8,128)(2,1)} %copy.21) | data formatting | bytes 2752512 | tf_op jit(solution)/shard_map/convert_element_type | solution.py:57
  (4 shorter events, 0.0 us)
Async XLA Ops:
  6.5 3.3 %copy-start = (bf16[1,448,1536]{2,1,0:T(8,128)(2,1)S(1)}, bf16[1,448,1536]{2,1,0:T(8,128)(2,1)}, u32[]{:S(2)}) copy-start(bf16[1,448,1536]{2,1,0:T(8,128)(2,1)} %param.7) | copy-start | bytes 4128772
  6.5 144.7 %all-gather.2.cloned.1.call-start = ((), (), s32[]{:S(2)}) async-start(), calls=%async_computation.1 | async-start | bytes 15040512 | tf_op jit(solution)/shard_map/all_gather | solution.py:39
  12.2 7.8 %copy-start.4 = (s32[1,8,8]{2,1,0:T(8,128)S(1)}, s32[1,8,8]{2,1,0:T(8,128)}, u32[]{:S(2)}) copy-start(s32[1,8,8]{2,1,0:T(8,128)} %param.12) | copy-start | bytes 772
  12.2 7.8 %copy-start.5 = (s32[1,8,8]{2,1,0:T(8,128)S(1)}, s32[1,8,8]{2,1,0:T(8,128)}, u32[]{:S(2)}) copy-start(s32[1,8,8]{2,1,0:T(8,128)} %param.13) | copy-start | bytes 772
  13.5 67.2 %copy-start.2 = (f32[1536]{0:T(1024)S(1)}, f32[1536]{0:T(1024)}, u32[]{:S(2)}) copy-start(f32[1536]{0:T(1024)} %param.9) | copy-start | bytes 18436
  13.5 67.2 %copy-start.3 = (f32[1536]{0:T(1024)S(1)}, f32[1536]{0:T(1024)}, u32[]{:S(2)}) copy-start(f32[1536]{0:T(1024)} %param.8) | copy-start | bytes 18436
  13.5 66.3 %all-to-all-start = ((bf16[8,56,1536]{2,1,0:T(8,128)(2,1)}), bf16[8,56,1536]{2,1,0:T(8,128)(2,1)S(1)}, u32[]{:S(2)}, u32[]{:S(2)}) async-start(bf16[8,56,1536]{2,1,0:T(8,128)(2,1)} %select_select_fusion), calls=%async_computation | async-start | bytes 2752512 | tf_op jit(solution)/shard_map/all_to_all | solution.py:29
  20.2 131.0 %copy-start.6 = (f32[4608]{0:T(1024)S(1)}, f32[4608]{0:T(1024)}, u32[]{:S(2)}) copy-start(f32[4608]{0:T(1024)} %param.11) | copy-start | bytes 55300
  186.0 2.7 %copy-start.1 = (bf16[8,56,24,64]{3,2,1,0:T(8,128)(2,1)S(1)}, bf16[8,56,24,64]{3,2,1,0:T(8,128)(2,1)}, u32[]{:S(2)}) copy-start(bf16[8,56,24,64]{3,2,1,0:T(8,128)(2,1)} %reshape.237) | copy-start | bytes 4128772
Sparse Core Ops, SparseCore 0:
  9.7 141.5 all-gather.1
where the time goes:
time: 205 us; the launch traced here: 204 us
  waiting for transfers between devices  129 us (63%)
  local copies, waits for them, and re-layouts  25.9 us (13%)
  matrix products  21.3 us (10%)
  between operations  13.5 us (7%)
  other arithmetic  7.79 us (4%)
  starting transfers between devices  6.49 us (3%)
    all_gather x1, waiting for transfers between devices, on_device(): lax.all_gather(qkv_weight, ('dp', 'fsdp'), axis=1, tiled=True)  68.9 us
    all_to_all x1, waiting for transfers between devices, on_device(): lax.all_to_all(outgoing, 'dp', split_axis=0, concat_axis=0, tiled=True)  59.6 us
    dot_general x1, matrix products, on_device(): jnp.dot(normed, lax.all_gather(qkv_weight, ('dp', 'fsdp'), axis=1, tiled=...  15.1 us
    convert_element_type x2, local copies, waits for them, and re-layouts, on_device(): return context.reshape(1, n_dp * cap, width).astype(jnp.bfloat16)  6.56 us
    all_to_all x1, starting transfers between devices, on_device(): lax.all_to_all(outgoing, 'dp', split_axis=0, concat_axis=0, tiled=True)  6.49 us
    reshape x1, local copies, waits for them, and re-layouts, on_device(): query = qkv[:, :width].reshape(n_dp, cap, HEADS, HEAD)  4.43 us
    reshape x1, local copies, waits for them, and re-layouts, on_device(): keys = qkv[:, width:2 * width].reshape(n_dp, cap, HEADS, HEAD)  4.43 us
    dot_general x1, matrix products, on_device(): jnp.einsum('sqhe,skhe->shqk', query, keys, preferred_element_type=jnp.flo...  4.19 us
  transfers between devices with their start and end apart: 2, of which 2 were waited for; matrix products, arithmetic and copies ran while one was open for 4% of the time, Pallas kernels for 0%

commit v1 on v0

v1 whole, which is shorter than its diff:
```python
import functools

import jax
import jax.numpy as jnp
from jax import lax
from jax.experimental import pallas as pl
from jax.experimental.pallas import tpu as pltpu
from jax.sharding import PartitionSpec as P

HEAD = 64
GROUP = 4
COLS = HEAD * GROUP
BF16 = jnp.bfloat16
F32 = jnp.float32


def attend_kernel(n_images, cap, len_ref, got_ref, gain_ref, shift_ref, bq_ref, bk_ref, bv_ref, wq_ref, wk_ref, wv_ref, out_ref, normed):
    @pl.when(pl.program_id(0) == 0)
    def _():
        for s in range(n_images):
            x = got_ref[s].astype(F32)
            centred = x - jnp.mean(x, axis=1, keepdims=True)
            var = jnp.mean(centred * centred, axis=1, keepdims=True)
            y = centred * lax.rsqrt(var + 1e-06) * gain_ref[...] + shift_ref[...]
            normed[s * cap : (s + 1) * cap, :] = y

    rows = normed[...].astype(BF16)

    def project(w_ref, b_ref):
        y = lax.dot_general(rows, w_ref[...], (((1,), (1,)), ((), ())), preferred_element_type=F32)
        return (y + b_ref[...]).astype(BF16).astype(F32)

    q, k, v = project(wq_ref, bq_ref), project(wk_ref, bk_ref), project(wv_ref, bv_ref)
    lane_head = lax.broadcasted_iota(jnp.int32, (cap, COLS), 1) // HEAD
    key_at = lax.broadcasted_iota(jnp.int32, (GROUP * cap, cap), 1)
    row_at = lax.broadcasted_iota(jnp.int32, (cap, COLS), 0)
    for s in range(n_images):
        at = slice(s * cap, (s + 1) * cap)
        length = len_ref[s]
        stacked = jnp.concatenate([jnp.where(lane_head == h, q[at], 0.0) for h in range(GROUP)], axis=0)
        scores = lax.dot_general(stacked.astype(BF16), k[at].astype(BF16), (((1,), (1,)), ((), ())), preferred_element_type=F32)
        scores = jnp.where(key_at < length, scores * HEAD ** (-0.5), -1e30)
        expo = jnp.exp(scores - jnp.max(scores, axis=1, keepdims=True))
        probs = (expo / jnp.sum(expo, axis=1, keepdims=True)).astype(BF16)
        mixed = jnp.dot(probs, v[at].astype(BF16), preferred_element_type=F32)
        total = jnp.where(lane_head == 0, mixed[:cap], 0.0)
        for h in range(1, GROUP):
            total = jnp.where(lane_head == h, mixed[h * cap : (h + 1) * cap], total)
        out_ref[s] = jnp.where(row_at < length, total, 0.0).astype(BF16)


def attend(got, recv_len, gain, shift, weight_t, bias):
    n_images, cap, width = got.shape
    steps = width // COLS
    full = lambda shape: pl.BlockSpec(shape, lambda i: (0,) * len(shape))
    bias_spec = lambda part: pl.BlockSpec((1, COLS), lambda i: (0, part * steps + i))
    weight_spec = lambda part: pl.BlockSpec((COLS, width), lambda i: (part * steps + i, 0))
    bias = bias.reshape(1, -1)
    return pl.pallas_call(
        functools.partial(attend_kernel, n_images, cap),
        grid=(steps,),
        in_specs=[
            pl.BlockSpec(memory_space=pltpu.SMEM),
            full((n_images, cap, width)),
            full((1, width)),
            full((1, width)),
            bias_spec(0),
            bias_spec(1),
            bias_spec(2),
            weight_spec(0),
            weight_spec(1),
            weight_spec(2),
        ],
        out_specs=pl.BlockSpec((n_images, cap, COLS), lambda i: (0, 0, i)),
        out_shape=jax.ShapeDtypeStruct((n_images, cap, width), BF16),
        scratch_shapes=[pltpu.VMEM((n_images * cap, width), F32)],
        compiler_params=pltpu.CompilerParams(vmem_limit_bytes=48 * 2**20),
        cost_estimate=pl.CostEstimate(flops=2 * n_images * cap * width * 3 * width, bytes_accessed=3 * width * width * 2, transcendentals=0),
    )(recv_len, got, gain.reshape(1, -1), shift.reshape(1, -1), bias, bias, bias, weight_t, weight_t, weight_t)


def move(patches, qkv_weight, table_len, table_dest):
    n_dp = lax.axis_size("dp")
    me_dp = lax.axis_index("dp")
    cap, width = patches.shape[0] // n_dp, patches.shape[1]
    own_len = lax.dynamic_index_in_dim(table_len, me_dp, 0, keepdims=False)
    own_dest = lax.dynamic_index_in_dim(table_dest, me_dp, 0, keepdims=False)
    offsets = jnp.cumsum(own_len) - own_len
    onehot = own_dest[None, :] == jnp.arange(n_dp, dtype=jnp.int32)[:, None]
    slot_len = jnp.sum(jnp.where(onehot, own_len[None, :], 0), axis=1)
    slot_off = jnp.sum(jnp.where(onehot, offsets[None, :], 0), axis=1)
    position = jnp.arange(cap, dtype=jnp.int32)
    live = position[None, :] < slot_len[:, None]
    index = jnp.where(live, slot_off[:, None] + position[None, :], 0)
    picked = jnp.take(patches, index.reshape(-1), axis=0).reshape(n_dp, cap, width)
    outgoing = jnp.where(live[:, :, None], picked, jnp.zeros((), picked.dtype))
    got = lax.all_to_all(outgoing, "dp", split_axis=0, concat_axis=0, tiled=True)
    weight_t = lax.all_gather(qkv_weight.T, ("dp", "fsdp"), axis=0, tiled=True)
    return got, weight_t


def on_device(patches, ln_gain, ln_bias, qkv_weight, qkv_bias, lengths, destinations):
    me_dp = lax.axis_index("dp")
    table_len, table_dest = lengths[0], destinations[0]
    got, weight_t = move(patches[0], qkv_weight, table_len, table_dest)
    recv_len = jnp.sum(jnp.where(table_dest == me_dp, table_len, 0), axis=1)
    context = attend(got, recv_len, ln_gain, ln_bias, weight_t, qkv_bias)
    return context.reshape(1, -1, context.shape[2])


def solution(mesh):
    placed = (
        P(("group", "fsdp"), "dp", None),
        P(),
        P(),
        P(None, ("dp", "fsdp")),
        P(),
        P(("group", "fsdp"), None, None),
        P(("group", "fsdp"), None, None),
    )
    return jax.shard_map(
        on_device,
        mesh=mesh,
        in_specs=placed,
        out_specs=P(("group", "fsdp"), "dp", None),
        check_vma=False,
    )
```

time: 205 us -> 185 us (0.902)
  Pallas kernels: 0 us -> 26.3 us
  local copies, waits for them, and re-layouts: 25.9 us -> 3.76 us
  matrix products: 21.3 us -> 0 us
  other arithmetic: 7.79 us -> 2.62 us
  waiting for transfers between devices: 129 us -> 132 us
    pallas_call x0 -> x1, Pallas kernels: none -> 26.3 us  [attend(): pl.pallas_call(functools.partial(attend_kernel, n_images, cap), grid=(ste...]
    dot_general x3 -> x0, matrix products: 21.3 us -> none  [the longest x1 15.1 us: on_device(): jnp.dot(normed, lax.all_gather(qkv_weight, ('dp', 'fsdp'), axis=1, tiled=...]
    reshape x3, local copies, waits for them, and re-layouts: 11.5 us -> 0.03 us  [the longest x1 0.01 us: attend(): bias = bias.reshape(1, -1)]
    convert_element_type x2 -> x0, local copies, waits for them, and re-layouts: 6.56 us -> none  [on_device(): return context.reshape(1, n_dp * cap, width).astype(jnp.bfloat16)]
    slice x1 -> x0, local copies, waits for them, and re-layouts: 3.96 us -> none  [on_device(): values = qkv[:, 2 * width:].reshape(n_dp, cap, HEADS, HEAD)]
    sub x2 -> x1, other arithmetic: 3.37 us -> 0.69 us  [move(): offsets = jnp.cumsum(own_len) - own_len]
    all_gather x1, waiting for transfers between devices: 68.9 us -> 71.4 us  [move(): weight_t = lax.all_gather(qkv_weight.T, ('dp', 'fsdp'), axis=0, tiled=True)]
  transfers between devices with their start and end apart: 2 -> 2, of which waited for: 2 -> 2; matrix products, arithmetic and copies ran while one was open for 4% -> 3% of each run, Pallas kernels for 0% -> 0%
where the time goes in v1:
time: 185 us; the launch traced here: 184 us
  waiting for transfers between devices  132 us (71%)
  Pallas kernels  26.3 us (14%)
  between operations  13.5 us (7%)
  starting transfers between devices  6.5 us (4%)
  local copies, waits for them, and re-layouts  3.76 us (2%)
  other arithmetic  2.62 us (1%)
    all_gather x1, waiting for transfers between devices, move(): weight_t = lax.all_gather(qkv_weight.T, ('dp', 'fsdp'), axis=0, tiled=True)  71.4 us
    all_to_all x1, waiting for transfers between devices, move(): lax.all_to_all(outgoing, 'dp', split_axis=0, concat_axis=0, tiled=True)  59.7 us
    pallas_call x1, Pallas kernels, attend(): pl.pallas_call(functools.partial(attend_kernel, n_images, cap), grid=(ste...  26.3 us
    all_to_all x1, starting transfers between devices, move(): lax.all_to_all(outgoing, 'dp', split_axis=0, concat_axis=0, tiled=True)  6.5 us
  transfers between devices with their start and end apart: 2, of which 2 were waited for; matrix products, arithmetic and copies ran while one was open for 3% of the time, Pallas kernels for 0%

profile of v1, /device:TPU:1, one launch (start us, length us, event | category | flops | bytes accessed | tf_op | source)
XLA Modules:
  0.0 184.4 jit_solution(18328429525068590675)
XLA Ops:
  6.5 0.0 copy-start
  6.5 0.0 all-gather.2.cloned.1.call-start
  6.5 0.7 all-gather.2.cloned.1.call-update
  7.3 0.7 fusion
  8.0 0.2 reduce-window.8
  8.1 0.7 dynamic-slice_bitcast_fusion
  8.8 0.7 bitcast_subtract_fusion
  9.5 0.1 select_reduce_fusion.1
  9.7 0.1 add_select_fusion
  9.7 0.1 select_n.67
  9.9 0.0 copy-done
  9.9 2.2 %gather_fusion = bf16[448,1536]{1,0:T(8,128)(2,1)S(1)} fusion(bf16[448,1536]{1,0:T(8,128)(2,1)S(1)} %bitcast.14, s32[1024]{0:T(1024)S(1)} %pad_clamp_fusion), kind=kCustom, calls=%fused_computation | custom fusion | bytes 2754304 | tf_op jit(solution)/shard_map/jit(_take)/gather | solution.py:95
  12.1 0.1 iota_compare_fusion.1
  12.2 1.3 select_select_fusion
  13.5 0.0 copy-start.1
  13.5 0.0 copy-start.2
  13.5 0.0 copy-start.3
  13.5 0.0 copy-start.4
  13.5 0.0 copy-start.5
  13.5 6.5 %all-to-all-start = ((bf16[8,56,1536]{2,1,0:T(8,128)(2,1)}), bf16[8,56,1536]{2,1,0:T(8,128)(2,1)S(1)}, u32[]{:S(2)}, u32[]{:S(2)}) async-start(bf16[8,56,1536]{2,1,0:T(8,128)(2,1)} %select_select_fusion), calls=%async_computation | async-start | bytes 2752512 | tf_op jit(solution)/shard_map/all_to_all | solution.py:97
  20.0 0.0 copy-done.1
  20.1 0.0 copy-done.2
  20.1 0.0 copy-done.3
  20.1 0.0 copy-done.4
  20.1 0.0 copy-done.5
  20.1 0.1 select_reduce_fusion.2.len_ref
  20.2 59.7 %all-to-all-done.got_ref = bf16[8,56,1536]{2,1,0:T(8,128)(2,1)S(1)} async-done(((bf16[8,56,1536]{2,1,0:T(8,128)(2,1)}), bf16[8,56,1536]{2,1,0:T(8,128)(2,1)S(1)}, u32[]{:S(2)}, u32[]{:S(2)}) %all-to-all-start) | async-done | bytes 1376288 | tf_op jit(solution)/shard_map/all_to_all | solution.py:97
  79.9 71.4 %all-gather.2.cloned.1.call-done.wq_ref.wk_ref.wv_ref = bf16[4608,1536]{1,0:T(8,128)(2,1)} async-done(((bf16[288,1536]{1,0:T(8,128)(2,1)}), bf16[4608,1536]{1,0:T(8,128)(2,1)}) %all-gather.2.cloned.1.call-update) | async-done | bytes 14155792 | tf_op jit(solution)/shard_map/all_gather | solution.py:98
  151.3 26.3 %shard_map.73 = bf16[8,56,1536]{2,1,0:T(8,128)(2,1)} custom-call(s32[8]{0:T(128)S(1)} %select_reduce_fusion.2.len_ref, bf16[8,56,1536]{2,1,0:T(8,128)(2,1)S(1)} %all-to-all-done.got_ref, f32[1,1536]{1,0:T(1,128)S(1)} %reshape.150.gain_ref, f32[1,1536]{1,0:T(1,128)S(1)} %reshape.151.shift_ref, f32[1,4608]{1,0:T(1,128)S(1)} %reshape.152.bq_ref.bk_ref.bv_ref, ...), custom_call_target="tpu_custom_call" | custom-call | flops 6341787648 | bytes 14155776 | tf_op jit(solution)/shard_map/pallas_call | solution.py:59
  (5 shorter events, 0.0 us)
Async XLA Ops:
  6.5 3.3 %copy-start = (bf16[1,448,1536]{2,1,0:T(8,128)(2,1)S(1)}, bf16[1,448,1536]{2,1,0:T(8,128)(2,1)}, u32[]{:S(2)}) copy-start(bf16[1,448,1536]{2,1,0:T(8,128)(2,1)} %param.7) | copy-start | bytes 4128772
  6.5 144.7 %all-gather.2.cloned.1.call-start = ((), (), s32[]{:S(2)}) async-start(), calls=%async_computation.1 | async-start | bytes 15040512 | tf_op jit(solution)/shard_map/all_gather | solution.py:98
  13.5 6.5 %copy-start.1 = (f32[4608]{0:T(1024)S(1)}, f32[4608]{0:T(1024)}, u32[]{:S(2)}) copy-start(f32[4608]{0:T(1024)} %param.11) | copy-start | bytes 55300
  13.5 6.6 %copy-start.2 = (f32[1536]{0:T(1024)S(1)}, f32[1536]{0:T(1024)}, u32[]{:S(2)}) copy-start(f32[1536]{0:T(1024)} %param.8) | copy-start | bytes 18436
  13.5 6.6 %copy-start.3 = (f32[1536]{0:T(1024)S(1)}, f32[1536]{0:T(1024)}, u32[]{:S(2)}) copy-start(f32[1536]{0:T(1024)} %param.9) | copy-start | bytes 18436
  13.5 6.6 %copy-start.4 = (s32[1,8,8]{2,1,0:T(8,128)S(1)}, s32[1,8,8]{2,1,0:T(8,128)}, u32[]{:S(2)}) copy-start(s32[1,8,8]{2,1,0:T(8,128)} %param.12) | copy-start | bytes 772
  13.5 6.6 %copy-start.5 = (s32[1,8,8]{2,1,0:T(8,128)S(1)}, s32[1,8,8]{2,1,0:T(8,128)}, u32[]{:S(2)}) copy-start(s32[1,8,8]{2,1,0:T(8,128)} %param.13) | copy-start | bytes 772
  13.5 66.4 %all-to-all-start = ((bf16[8,56,1536]{2,1,0:T(8,128)(2,1)}), bf16[8,56,1536]{2,1,0:T(8,128)(2,1)S(1)}, u32[]{:S(2)}, u32[]{:S(2)}) async-start(bf16[8,56,1536]{2,1,0:T(8,128)(2,1)} %select_select_fusion), calls=%async_computation | async-start | bytes 2752512 | tf_op jit(solution)/shard_map/all_to_all | solution.py:97
Sparse Core Ops, SparseCore 0:
  9.7 141.5 all-gather.1

commit v2 on v1

--- a/solution.py
+++ b/solution.py
@@ -99,10 +99,201 @@
     return got, weight_t
 
 
+MESH = pl.DeviceIdType.MESH
+PARTS = 3
+
+
+def move_kernel(n_dp, cap, len_ref, dest_ref, rows_ref, shard_ref, got_ref, all_ref, outgoing, up_sem, down_sem, x_sem, y_sem, core_sem, ring_in, core_in, image_out, image_in, local_sem):
+    group, dp, core = lax.axis_index("group"), lax.axis_index("dp"), lax.axis_index("fsdp")
+    nz = n_dp // 2
+    z = dp // 2
+    across = dp + 1 - 2 * (dp % 2)
+    own_parts = (2 * group, 1)
+    other_part = 2 - 2 * group
+    replica = (1 - group, dp, core)
+    mate = (group, dp, 1 - core)
+
+    barrier = pltpu.get_barrier_semaphore()
+    for j in range(1, n_dp):
+        pl.semaphore_signal(barrier, inc=1, device_id=(group, (dp + j) % n_dp, core), device_id_type=MESH)
+    pl.semaphore_signal(barrier, inc=1, device_id=replica, device_id_type=MESH)
+    pl.semaphore_signal(barrier, inc=1, device_id=mate, device_id_type=MESH)
+    pl.semaphore_wait(barrier, n_dp + 1)
+
+    sent = []
+
+    def send(sems, into, who, part, device, own, *conditions):
+        def copy():
+            return pltpu.make_async_remote_copy(
+                src_ref=shard_ref.at[part] if own else all_ref.at[who, core, part],
+                dst_ref=all_ref.at[who, core, part],
+                send_sem=sems.at[who, part],
+                recv_sem=into.at[who, part],
+                device_id=device,
+                device_id_type=MESH,
+            )
+
+        when(conditions, lambda: copy().start())
+        sent.append((conditions, lambda: copy().wait_send()))
+
+    def when(conditions, do):
+        if conditions:
+            pl.when(conditions[0])(lambda: when(conditions[1:], do))
+        else:
+            do()
+
+    def arrive(sems, who, of_core, part, *conditions):
+        def wait():
+            pltpu.make_async_remote_copy(
+                src_ref=all_ref.at[who, of_core, part],
+                dst_ref=all_ref.at[who, of_core, part],
+                send_sem=y_sem.at[who, part],
+                recv_sem=sems.at[who, part],
+                device_id=mate,
+                device_id_type=MESH,
+            ).wait_recv()
+
+        when(conditions, wait)
+
+    for part in own_parts:
+        send(up_sem, ring_in, dp, part, (group, dp + 2, core), True, z < nz - 1)
+        send(down_sem, ring_in, dp, part, (group, dp - 2, core), True, z > 0)
+        send(x_sem, ring_in, dp, part, (group, across, core), True)
+
+    own_dest = [dest_ref[dp, i] for i in range(n_dp)]
+    own_len = [len_ref[dp, i] for i in range(n_dp)]
+    row_at = lax.broadcasted_iota(jnp.int32, (cap, n_dp * cap), 0)
+    column_at = lax.broadcasted_iota(jnp.int32, (cap, n_dp * cap), 1)
+    picks = []
+    for j in range(n_dp):
+        to = (dp + j) % n_dp
+        length, offset, start = jnp.int32(0), jnp.int32(0), jnp.int32(0)
+        for i in range(n_dp):
+            length = jnp.where(own_dest[i] == to, own_len[i], length)
+            offset = jnp.where(own_dest[i] == to, start, offset)
+            start = start + own_len[i]
+        picks.append(jnp.where((row_at < length) & (column_at == row_at + offset), 1.0, 0.0))
+    pick = jnp.concatenate(picks, axis=0).astype(BF16)
+    picked = jnp.dot(pick, rows_ref[...], preferred_element_type=F32)
+    for j in range(n_dp):
+        outgoing[j] = picked[j * cap : (j + 1) * cap].astype(BF16)
+
+    def image(j):
+        return pltpu.make_async_remote_copy(
+            src_ref=outgoing.at[j],
+            dst_ref=got_ref.at[dp],
+            send_sem=image_out.at[j],
+            recv_sem=image_in.at[j],
+            device_id=(group, (dp + j) % n_dp, core),
+            device_id_type=MESH,
+        )
+
+    def image_arrival(j):
+        source = (dp + n_dp - j) % n_dp
+        return pltpu.make_async_remote_copy(
+            src_ref=outgoing.at[j],
+            dst_ref=got_ref.at[source],
+            send_sem=image_out.at[j],
+            recv_sem=image_in.at[j],
+            device_id=(group, source, core),
+            device_id_type=MESH,
+        )
+
+    for j in range(1, n_dp):
+        image(j).start()
+    own_image = pltpu.make_async_copy(outgoing.at[0], got_ref.at[dp], local_sem.at[0])
+    own_image.start()
+    own_shard = pltpu.make_async_copy(shard_ref, all_ref.at[dp, core], local_sem.at[1])
+    own_shard.start()
+    for part in range(PARTS):
+        send(core_sem, core_in, dp, part, mate, True)
+
+    def sides(d):
+        if d == 0:
+            return [((), 0, 0)]
+        return [((z >= d,), -2 * d, 1), ((z < nz - d,), 2 * d, -1)]
+
+    def from_z(d):
+        for at, part in enumerate(own_parts):
+            for valid, step, way in sides(d):
+                who = dp + step
+                arrive(ring_in, who, core, part, *valid)
+                if way == 1:
+                    send(up_sem, ring_in, who, part, (group, dp + 2, core), False, *valid, z < nz - 1)
+                else:
+                    send(down_sem, ring_in, who, part, (group, dp - 2, core), False, *valid, z > 0)
+                send(x_sem, ring_in, who, part, (group, across, core), False, *valid)
+                if at == 0:
+                    send(y_sem, ring_in, who, part, replica, False, *valid)
+                send(core_sem, core_in, who, part, mate, False, *valid)
+
+    def from_x(d):
+        for at, part in enumerate(own_parts):
+            for valid, step, _ in sides(d):
+                who = across + step
+                arrive(ring_in, who, core, part, *valid)
+                if at == 0:
+                    send(y_sem, ring_in, who, part, replica, False, *valid)
+                send(core_sem, core_in, who, part, mate, False, *valid)
+
+    def from_y(d, base):
+        for valid, step, _ in sides(d):
+            arrive(ring_in, base + step, core, other_part, *valid)
+            send(core_sem, core_in, base + step, other_part, mate, False, *valid)
+
+    for d in range(1, nz + 2):
+        if d < nz:
+            from_z(d)
+        if d <= nz:
+            from_x(d - 1)
+        if 2 <= d <= nz:
+            from_y(d - 1, dp)
+        if d >= 2:
+            from_y(d - 2, across)
+
+    for who in range(n_dp):
+        for part in range(PARTS):
+            arrive(core_in, who, 1 - core, part)
+    for j in range(1, n_dp):
+        image_arrival(j).wait_recv()
+    for conditions, wait in sent:
+        when(conditions, wait)
+    for j in range(1, n_dp):
+        image(j).wait_send()
+    own_image.wait()
+    own_shard.wait()
+
+
+def move_by_copies(patches, qkv_weight, table_len, table_dest):
+    n_dp, n_core = lax.axis_size("dp"), lax.axis_size("fsdp")
+    cap, width = patches.shape[0] // n_dp, patches.shape[1]
+    columns = qkv_weight.shape[1]
+    shard = qkv_weight.T.reshape(PARTS, columns // PARTS, width)
+    dma = pltpu.SemaphoreType.DMA
+    got, gathered = pl.pallas_call(
+        functools.partial(move_kernel, n_dp, cap),
+        in_specs=[
+            pl.BlockSpec(memory_space=pltpu.SMEM),
+            pl.BlockSpec(memory_space=pltpu.SMEM),
+            pl.BlockSpec(memory_space=pltpu.VMEM),
+            pl.BlockSpec(memory_space=pl.ANY),
+        ],
+        out_specs=[pl.BlockSpec(memory_space=pl.ANY)] * 2,
+        out_shape=[
+            jax.ShapeDtypeStruct((n_dp, cap, width), BF16),
+            jax.ShapeDtypeStruct((n_dp, n_core, PARTS, columns // PARTS, width), BF16),
+        ],
+        scratch_shapes=[pltpu.VMEM((n_dp, cap, width), BF16)] + [dma((n_dp, PARTS))] * 7 + [dma((n_dp,))] * 2 + [dma((2,))],
+        compiler_params=pltpu.CompilerParams(collective_id=0, has_side_effects=True, vmem_limit_bytes=40 * 2**20),
+    )(table_len, table_dest, patches, shard)
+    return got, gathered.reshape(n_dp * n_core * columns, width)
+
+
 def on_device(patches, ln_gain, ln_bias, qkv_weight, qkv_bias, lengths, destinations):
     me_dp = lax.axis_index("dp")
     table_len, table_dest = lengths[0], destinations[0]
-    got, weight_t = move(patches[0], qkv_weight, table_len, table_dest)
+    by_copies = lax.axis_size("fsdp") == 2 and lax.axis_size("group") == 2 and lax.axis_size("dp") % 2 == 0
+    got, weight_t = (move_by_copies if by_copies else move)(patches[0], qkv_weight, table_len, table_dest)
     recv_len = jnp.sum(jnp.where(table_dest == me_dp, table_len, 0), axis=1)
     context = attend(got, recv_len, ln_gain, ln_bias, weight_t, qkv_bias)
     return context.reshape(1, -1, context.shape[2])

time: 185 us -> 120 us (0.65)
  waiting for transfers between devices: 132 us -> 0 us
  Pallas kernels: 26.3 us -> 113 us
  between operations: 13.5 us -> 0.03 us
  starting transfers between devices: 6.5 us -> 0 us
  local copies, waits for them, and re-layouts: 3.76 us -> 6.02 us
    pallas_call x0 -> x1, Pallas kernels: none -> 86.6 us  [move_by_copies(): pl.pallas_call(functools.partial(move_kernel, n_dp, cap), in_specs=[pl.Bl...]
    all_gather x1 -> x0, waiting for transfers between devices: 71.4 us -> none  [move(): weight_t = lax.all_gather(qkv_weight.T, ('dp', 'fsdp'), axis=0, tiled=True)]
    all_to_all x1 -> x0, waiting for transfers between devices: 59.7 us -> none  [move(): lax.all_to_all(outgoing, 'dp', split_axis=0, concat_axis=0, tiled=True)]
    all_to_all x1 -> x0, starting transfers between devices: 6.5 us -> none  [move(): lax.all_to_all(outgoing, 'dp', split_axis=0, concat_axis=0, tiled=True)]
    unnamed x12 -> x8, local copies, waits for them, and re-layouts: 0.03 us -> 3.87 us
    gather x1 -> x0, local copies, waits for them, and re-layouts: 2.23 us -> none  [move(): jnp.take(patches, index.reshape(-1), axis=0).reshape(n_dp, cap, width)]
  transfers between devices with their start and end apart: 2 -> 0, of which waited for: 2 -> 0; matrix products, arithmetic and copies ran while one was open for 3% -> 0% of each run, Pallas kernels for 0% -> 0%
where the time goes in v2:
time: 120 us
  Pallas kernels  113 us (94%)
  local copies, waits for them, and re-layouts  6.02 us (5%)
    pallas_call x1, Pallas kernels, move_by_copies(): pl.pallas_call(functools.partial(move_kernel, n_dp, cap), in_specs=[pl.Bl...  86.6 us
    pallas_call x1, Pallas kernels, attend(): pl.pallas_call(functools.partial(attend_kernel, n_images, cap), grid=(ste...  26.3 us
    unnamed x8, local copies, waits for them, and re-layouts  3.87 us

profile of v2, /device:TPU:1, one launch (start us, length us, event | category | flops | bytes accessed | tf_op | source)
XLA Modules:
  0.0 119.8 jit_solution(15398641563965699742)
XLA Ops:
  0.0 0.8 select_reduce_fusion.len_ref
  0.8 0.7 reshape.19.gain_ref
  1.5 0.7 reshape.20.shift_ref
  2.2 0.7 reshape.21.bq_ref.bk_ref.bv_ref
  3.0 0.0 copy-start
  3.0 1.3 %copy-done = bf16[1,448,1536]{2,1,0:T(8,128)(2,1)S(1)} copy-done((bf16[1,448,1536]{2,1,0:T(8,128)(2,1)S(1)}, bf16[1,448,1536]{2,1,0:T(8,128)(2,1)}, u32[]{:S(2)}) %copy-start) | copy-done | bytes 1376280
  4.3 0.0 copy-start.1
  4.3 1.2 copy-done.1
  5.5 0.0 copy-start.2
  5.5 0.7 copy-done.2
  6.2 0.0 copy-start.3
  6.2 0.7 copy-done.3
  6.9 86.6 %shard_map.73 = (bf16[8,56,1536]{2,1,0:T(8,128)(2,1)S(1)}, bf16[8,2,3,96,1536]{4,3,2,1,0:T(8,128)(2,1)}) custom-call(s32[8,8]{1,0:T(8,128)S(1)} %bitcast.12, s32[8,8]{1,0:T(8,128)S(1)} %bitcast.13, bf16[448,1536]{1,0:T(8,128)(2,1)S(1)} %bitcast.10, bf16[3,96,1536]{2,1,0:T(8,128)(2,1)S(1)} %bitcast.11), custom_call_target="tpu_custom_call" | custom-call | tf_op jit(solution)/shard_map/pallas_call | solution.py:273
  93.4 26.3 %shard_map.74 = bf16[8,56,1536]{2,1,0:T(8,128)(2,1)} custom-call(s32[8]{0:T(128)S(1)} %select_reduce_fusion.len_ref, bf16[8,56,1536]{2,1,0:T(8,128)(2,1)S(1)} %get-tuple-element.7.got_ref, f32[1,1536]{1,0:T(1,128)S(1)} %reshape.19.gain_ref, f32[1,1536]{1,0:T(1,128)S(1)} %reshape.20.shift_ref, f32[1,4608]{1,0:T(1,128)S(1)} %reshape.21.bq_ref.bk_ref.bv_ref, ...), custom_call_target="tpu_custom_call" | custom-call | flops 6341787648 | bytes 14155776 | tf_op jit(solution)/shard_map/pallas_call | solution.py:59
Async XLA Ops:
  3.0 1.3 %copy-start = (bf16[1,448,1536]{2,1,0:T(8,128)(2,1)S(1)}, bf16[1,448,1536]{2,1,0:T(8,128)(2,1)}, u32[]{:S(2)}) copy-start(bf16[1,448,1536]{2,1,0:T(8,128)(2,1)} %param.7) | copy-start | bytes 4128772
  4.3 1.2 copy-start.1
  5.5 0.7 copy-start.2
  6.2 0.7 copy-start.3

commit v3 on v2

--- a/solution.py
+++ b/solution.py
@@ -14,56 +14,64 @@
 F32 = jnp.float32
 
 
-def attend_kernel(n_images, cap, len_ref, got_ref, gain_ref, shift_ref, bq_ref, bk_ref, bv_ref, wq_ref, wk_ref, wv_ref, out_ref, normed):
+def attend_kernel(n_images, cap, table_len_ref, table_dest_ref, got_ref, gain_ref, shift_ref, bq_ref, bk_ref, bv_ref, wq_ref, wk_ref, wv_ref, out_ref, normed, len_ref):
     @pl.when(pl.program_id(0) == 0)
     def _():
+        me = lax.axis_index("dp")
         for s in range(n_images):
-            x = got_ref[s].astype(F32)
-            centred = x - jnp.mean(x, axis=1, keepdims=True)
-            var = jnp.mean(centred * centred, axis=1, keepdims=True)
-            y = centred * lax.rsqrt(var + 1e-06) * gain_ref[...] + shift_ref[...]
-            normed[s * cap : (s + 1) * cap, :] = y
-
-    rows = normed[...].astype(BF16)
+            length = jnp.int32(0)
+            for j in range(n_images):
+                length = length + jnp.where(table_dest_ref[s, j] == me, table_len_ref[s, j], 0)
+            len_ref[s] = length
+        gain, shift = gain_ref[...][None, :], shift_ref[...][None, :]
+        for s in range(0, n_images, 2):
+            pair = []
+            for x in (got_ref[s].astype(F32), got_ref[s + 1].astype(F32)):
+                centred = x - jnp.mean(x, axis=1, keepdims=True)
+                var = jnp.mean(centred * centred, axis=1, keepdims=True)
+                pair.append(centred * lax.rsqrt(var + 1e-06) * gain + shift)
+            normed[s * cap : (s + 2) * cap, :] = jnp.concatenate(pair, axis=0).astype(BF16)
+
+    rows = normed[...]
 
     def project(w_ref, b_ref):
         y = lax.dot_general(rows, w_ref[...], (((1,), (1,)), ((), ())), preferred_element_type=F32)
-        return (y + b_ref[...]).astype(BF16).astype(F32)
+        return (y + b_ref[...][None, :]).astype(BF16).astype(F32)
 
     q, k, v = project(wq_ref, bq_ref), project(wk_ref, bk_ref), project(wv_ref, bv_ref)
     lane_head = lax.broadcasted_iota(jnp.int32, (cap, COLS), 1) // HEAD
-    key_at = lax.broadcasted_iota(jnp.int32, (GROUP * cap, cap), 1)
+    key_at = lax.broadcasted_iota(jnp.int32, (cap, GROUP * cap), 0)
     row_at = lax.broadcasted_iota(jnp.int32, (cap, COLS), 0)
     for s in range(n_images):
         at = slice(s * cap, (s + 1) * cap)
         length = len_ref[s]
         stacked = jnp.concatenate([jnp.where(lane_head == h, q[at], 0.0) for h in range(GROUP)], axis=0)
-        scores = lax.dot_general(stacked.astype(BF16), k[at].astype(BF16), (((1,), (1,)), ((), ())), preferred_element_type=F32)
+        scores = lax.dot_general(k[at].astype(BF16), stacked.astype(BF16), (((1,), (1,)), ((), ())), preferred_element_type=F32)
         scores = jnp.where(key_at < length, scores * HEAD ** (-0.5), -1e30)
-        expo = jnp.exp(scores - jnp.max(scores, axis=1, keepdims=True))
-        probs = (expo / jnp.sum(expo, axis=1, keepdims=True)).astype(BF16)
-        mixed = jnp.dot(probs, v[at].astype(BF16), preferred_element_type=F32)
+        expo = jnp.exp(scores - jnp.max(scores, axis=0, keepdims=True))
+        probs = (expo * (1.0 / jnp.sum(expo, axis=0, keepdims=True))).astype(BF16)
+        mixed = lax.dot_general(probs, v[at].astype(BF16), (((0,), (0,)), ((), ())), preferred_element_type=F32)
         total = jnp.where(lane_head == 0, mixed[:cap], 0.0)
         for h in range(1, GROUP):
             total = jnp.where(lane_head == h, mixed[h * cap : (h + 1) * cap], total)
         out_ref[s] = jnp.where(row_at < length, total, 0.0).astype(BF16)
 
 
-def attend(got, recv_len, gain, shift, weight_t, bias):
+def attend(got, table_len, table_dest, gain, shift, weight_t, bias):
     n_images, cap, width = got.shape
     steps = width // COLS
     full = lambda shape: pl.BlockSpec(shape, lambda i: (0,) * len(shape))
-    bias_spec = lambda part: pl.BlockSpec((1, COLS), lambda i: (0, part * steps + i))
+    bias_spec = lambda part: pl.BlockSpec((COLS,), lambda i: (part * steps + i,))
     weight_spec = lambda part: pl.BlockSpec((COLS, width), lambda i: (part * steps + i, 0))
-    bias = bias.reshape(1, -1)
     return pl.pallas_call(
         functools.partial(attend_kernel, n_images, cap),
         grid=(steps,),
         in_specs=[
             pl.BlockSpec(memory_space=pltpu.SMEM),
+            pl.BlockSpec(memory_space=pltpu.SMEM),
             full((n_images, cap, width)),
-            full((1, width)),
-            full((1, width)),
+            full((width,)),
+            full((width,)),
             bias_spec(0),
             bias_spec(1),
             bias_spec(2),
@@ -73,10 +81,10 @@
         ],
         out_specs=pl.BlockSpec((n_images, cap, COLS), lambda i: (0, 0, i)),
         out_shape=jax.ShapeDtypeStruct((n_images, cap, width), BF16),
-        scratch_shapes=[pltpu.VMEM((n_images * cap, width), F32)],
+        scratch_shapes=[pltpu.VMEM((n_images * cap, width), BF16), pltpu.SMEM((n_images,), jnp.int32)],
         compiler_params=pltpu.CompilerParams(vmem_limit_bytes=48 * 2**20),
         cost_estimate=pl.CostEstimate(flops=2 * n_images * cap * width * 3 * width, bytes_accessed=3 * width * width * 2, transcendentals=0),
-    )(recv_len, got, gain.reshape(1, -1), shift.reshape(1, -1), bias, bias, bias, weight_t, weight_t, weight_t)
+    )(table_len, table_dest, got, gain, shift, bias, bias, bias, weight_t, weight_t, weight_t)
 
 
 def move(patches, qkv_weight, table_len, table_dest):
@@ -290,12 +298,10 @@
 
 
 def on_device(patches, ln_gain, ln_bias, qkv_weight, qkv_bias, lengths, destinations):
-    me_dp = lax.axis_index("dp")
     table_len, table_dest = lengths[0], destinations[0]
     by_copies = lax.axis_size("fsdp") == 2 and lax.axis_size("group") == 2 and lax.axis_size("dp") % 2 == 0
     got, weight_t = (move_by_copies if by_copies else move)(patches[0], qkv_weight, table_len, table_dest)
-    recv_len = jnp.sum(jnp.where(table_dest == me_dp, table_len, 0), axis=1)
-    context = attend(got, recv_len, ln_gain, ln_bias, weight_t, qkv_bias)
+    context = attend(got, table_len, table_dest, ln_gain, ln_bias, weight_t, qkv_bias)
     return context.reshape(1, -1, context.shape[2])
 
 

time: 120 us -> 117 us (0.975)
  local copies, waits for them, and re-layouts: 6.02 us -> 3.91 us
    reshape x3 -> x0, local copies, waits for them, and re-layouts: 2.14 us -> none  [the longest x1 0.74 us: attend(): bias = bias.reshape(1, -1)]
    unnamed x8 -> x18, local copies, waits for them, and re-layouts: 3.87 us -> 3.91 us
where the time goes in v3:
time: 117 us
  Pallas kernels  113 us (97%)
  local copies, waits for them, and re-layouts  3.91 us (3%)
    pallas_call x1, Pallas kernels, move_by_copies(): pl.pallas_call(functools.partial(move_kernel, n_dp, cap), in_specs=[pl.Bl...  86.6 us
    pallas_call x1, Pallas kernels, attend(): pl.pallas_call(functools.partial(attend_kernel, n_images, cap), grid=(ste...  26.5 us
    unnamed x18, local copies, waits for them, and re-layouts  3.91 us

profile of v3, /device:TPU:1, one launch (start us, length us, event | category | flops | bytes accessed | tf_op | source)
XLA Modules:
  0.0 117.1 jit_solution(6577985217084576679)
XLA Ops:
  0.0 0.0 copy-start.4
  0.0 0.0 copy-start
  0.0 1.4 %copy-done = bf16[1,448,1536]{2,1,0:T(8,128)(2,1)S(1)} copy-done((bf16[1,448,1536]{2,1,0:T(8,128)(2,1)S(1)}, bf16[1,448,1536]{2,1,0:T(8,128)(2,1)}, u32[]{:S(2)}) %copy-start) | copy-done | bytes 1376280
  1.4 0.0 copy-start.1
  1.4 1.2 copy-done.1
  2.5 0.0 copy-start.3
  2.5 0.7 copy-done.3
  3.2 0.0 copy-start.5
  3.2 0.7 copy-done.5
  3.9 0.0 copy-start.2
  3.9 0.0 copy-start.6
  3.9 0.0 copy-start.7
  3.9 0.0 copy-start.8
  3.9 86.6 %shard_map.73 = (bf16[8,56,1536]{2,1,0:T(8,128)(2,1)S(1)}, bf16[8,2,3,96,1536]{4,3,2,1,0:T(8,128)(2,1)}) custom-call(s32[8,8]{1,0:T(8,128)S(1)} %bitcast.10, s32[8,8]{1,0:T(8,128)S(1)} %bitcast.12, bf16[448,1536]{1,0:T(8,128)(2,1)S(1)} %bitcast.8, bf16[3,96,1536]{2,1,0:T(8,128)(2,1)S(1)} %bitcast.9), custom_call_target="tpu_custom_call" | custom-call | tf_op jit(solution)/shard_map/pallas_call | solution.py:281
  90.5 0.0 copy-done.4
  90.5 0.0 copy-done.2
  90.5 0.0 copy-done.6
  90.5 0.0 copy-done.7
  90.5 0.0 copy-done.8
  90.5 26.5 %shard_map.74 = bf16[8,56,1536]{2,1,0:T(8,128)(2,1)} custom-call(s32[8,8]{1,0:T(8,128)S(1)} %bitcast.11, s32[8,8]{1,0:T(8,128)S(1)} %bitcast.13, bf16[8,56,1536]{2,1,0:T(8,128)(2,1)S(1)} %get-tuple-element.7.got_ref, f32[1536]{0:T(1024)S(1)} %copy-done.7, f32[1536]{0:T(1024)S(1)} %copy-done.8, f32[4608]{0:T(1024)S(1)} %copy-done.2, f32[4608]{0:T(1024)S(1)} %copy-done.2, ...), custom_call_target="tpu_custom_call" | custom-call | flops 6341787648 | bytes 14155776 | tf_op jit(solution)/shard_map/pallas_call | solution.py:66
Async XLA Ops:
  0.0 90.5 %copy-start.4 = (s32[1,8,8]{2,1,0:T(8,128)S(1)}, s32[1,8,8]{2,1,0:T(8,128)}, u32[]{:S(2)}) copy-start(s32[1,8,8]{2,1,0:T(8,128)} %param.12) | copy-start | bytes 772
  0.0 1.4 %copy-start = (bf16[1,448,1536]{2,1,0:T(8,128)(2,1)S(1)}, bf16[1,448,1536]{2,1,0:T(8,128)(2,1)}, u32[]{:S(2)}) copy-start(bf16[1,448,1536]{2,1,0:T(8,128)(2,1)} %param.7) | copy-start | bytes 4128772
  1.4 1.2 copy-start.1
  2.5 0.7 copy-start.3
  3.2 0.7 copy-start.5
  3.9 86.6 %copy-start.2 = (f32[4608]{0:T(1024)S(1)}, f32[4608]{0:T(1024)}, u32[]{:S(2)}) copy-start(f32[4608]{0:T(1024)} %bv_ref.1) | copy-start | bytes 55300
  3.9 86.6 %copy-start.6 = (s32[1,8,8]{2,1,0:T(8,128)S(1)}, s32[1,8,8]{2,1,0:T(8,128)}, u32[]{:S(2)}) copy-start(s32[1,8,8]{2,1,0:T(8,128)} %param.13) | copy-start | bytes 772
  3.9 86.6 %copy-start.7 = (f32[1536]{0:T(1024)S(1)}, f32[1536]{0:T(1024)}, u32[]{:S(2)}) copy-start(f32[1536]{0:T(1024)} %gain_ref.1) | copy-start | bytes 18436
  3.9 86.6 %copy-start.8 = (f32[1536]{0:T(1024)S(1)}, f32[1536]{0:T(1024)}, u32[]{:S(2)}) copy-start(f32[1536]{0:T(1024)} %shift_ref.1) | copy-start | bytes 18436

commit v4 on v3

--- a/solution.py
+++ b/solution.py
@@ -144,6 +144,9 @@
         when(conditions, lambda: copy().start())
         sent.append((conditions, lambda: copy().wait_send()))
 
+    def by_x(at, d):
+        return () if at == 0 else ((z + d) % 2 == group,)
+
     def when(conditions, do):
         if conditions:
             pl.when(conditions[0])(lambda: when(conditions[1:], do))
@@ -163,10 +166,10 @@
 
         when(conditions, wait)
 
-    for part in own_parts:
+    for at, part in enumerate(own_parts):
         send(up_sem, ring_in, dp, part, (group, dp + 2, core), True, z < nz - 1)
         send(down_sem, ring_in, dp, part, (group, dp - 2, core), True, z > 0)
-        send(x_sem, ring_in, dp, part, (group, across, core), True)
+        send(x_sem, ring_in, dp, part, (group, across, core), True, *by_x(at, 0))
 
     own_dest = [dest_ref[dp, i] for i in range(n_dp)]
     own_len = [len_ref[dp, i] for i in range(n_dp)]
@@ -230,7 +233,7 @@
                     send(up_sem, ring_in, who, part, (group, dp + 2, core), False, *valid, z < nz - 1)
                 else:
                     send(down_sem, ring_in, who, part, (group, dp - 2, core), False, *valid, z > 0)
-                send(x_sem, ring_in, who, part, (group, across, core), False, *valid)
+                send(x_sem, ring_in, who, part, (group, across, core), False, *valid, *by_x(at, d))
                 if at == 0:
                     send(y_sem, ring_in, who, part, replica, False, *valid)
                 send(core_sem, core_in, who, part, mate, False, *valid)
@@ -239,15 +242,20 @@
         for at, part in enumerate(own_parts):
             for valid, step, _ in sides(d):
                 who = across + step
+                valid = valid + by_x(at, d)
                 arrive(ring_in, who, core, part, *valid)
-                if at == 0:
-                    send(y_sem, ring_in, who, part, replica, False, *valid)
+                send(y_sem, ring_in, who, part, replica, False, *valid)
                 send(core_sem, core_in, who, part, mate, False, *valid)
 
     def from_y(d, base):
         for valid, step, _ in sides(d):
-            arrive(ring_in, base + step, core, other_part, *valid)
-            send(core_sem, core_in, base + step, other_part, mate, False, *valid)
+            who = base + step
+            arrive(ring_in, who, core, other_part, *valid)
+            send(core_sem, core_in, who, other_part, mate, False, *valid)
+            if base is across:
+                valid = valid + ((z + d) % 2 != group,)
+                arrive(ring_in, who, core, 1, *valid)
+                send(core_sem, core_in, who, 1, mate, False, *valid)
 
     for d in range(1, nz + 2):
         if d < nz:

time: 117 us -> 129 us (1.10)
  Pallas kernels: 113 us -> 125 us
    pallas_call x1, Pallas kernels: 86.6 us -> 98.1 us  [move_by_copies(): pl.pallas_call(functools.partial(move_kernel, n_dp, cap), in_specs=[pl.Bl...]
where the time goes in v4:
time: 129 us
  Pallas kernels  125 us (97%)
  local copies, waits for them, and re-layouts  3.91 us (3%)
    pallas_call x1, Pallas kernels, move_by_copies(): pl.pallas_call(functools.partial(move_kernel, n_dp, cap), in_specs=[pl.Bl...  98.1 us
    pallas_call x1, Pallas kernels, attend(): pl.pallas_call(functools.partial(attend_kernel, n_images, cap), grid=(ste...  26.5 us
    unnamed x18, local copies, waits for them, and re-layouts  3.91 us

profile of v4, /device:TPU:1, one launch (start us, length us, event | category | flops | bytes accessed | tf_op | source)
XLA Modules:
  0.0 128.6 jit_solution(17482244422824066340)
XLA Ops:
  0.0 0.0 copy-start.4
  0.0 0.0 copy-start
  0.0 1.4 %copy-done = bf16[1,448,1536]{2,1,0:T(8,128)(2,1)S(1)} copy-done((bf16[1,448,1536]{2,1,0:T(8,128)(2,1)S(1)}, bf16[1,448,1536]{2,1,0:T(8,128)(2,1)}, u32[]{:S(2)}) %copy-start) | copy-done | bytes 1376280
  1.4 0.0 copy-start.1
  1.4 1.2 copy-done.1
  2.5 0.0 copy-start.3
  2.5 0.7 copy-done.3
  3.2 0.0 copy-start.5
  3.2 0.7 copy-done.5
  3.9 0.0 copy-start.2
  3.9 0.0 copy-start.6
  3.9 0.0 copy-start.7
  3.9 0.0 copy-start.8
  3.9 98.1 %shard_map.73 = (bf16[8,56,1536]{2,1,0:T(8,128)(2,1)S(1)}, bf16[8,2,3,96,1536]{4,3,2,1,0:T(8,128)(2,1)}) custom-call(s32[8,8]{1,0:T(8,128)S(1)} %bitcast.10, s32[8,8]{1,0:T(8,128)S(1)} %bitcast.12, bf16[448,1536]{1,0:T(8,128)(2,1)S(1)} %bitcast.8, bf16[3,96,1536]{2,1,0:T(8,128)(2,1)S(1)} %bitcast.9), custom_call_target="tpu_custom_call" | custom-call | tf_op jit(solution)/shard_map/pallas_call | solution.py:289
  102.0 0.0 copy-done.4
  102.0 0.0 copy-done.2
  102.1 0.0 copy-done.6
  102.1 0.0 copy-done.7
  102.1 0.0 copy-done.8
  102.1 26.5 %shard_map.74 = bf16[8,56,1536]{2,1,0:T(8,128)(2,1)} custom-call(s32[8,8]{1,0:T(8,128)S(1)} %bitcast.11, s32[8,8]{1,0:T(8,128)S(1)} %bitcast.13, bf16[8,56,1536]{2,1,0:T(8,128)(2,1)S(1)} %get-tuple-element.7.got_ref, f32[1536]{0:T(1024)S(1)} %copy-done.7, f32[1536]{0:T(1024)S(1)} %copy-done.8, f32[4608]{0:T(1024)S(1)} %copy-done.2, f32[4608]{0:T(1024)S(1)} %copy-done.2, ...), custom_call_target="tpu_custom_call" | custom-call | flops 6341787648 | bytes 14155776 | tf_op jit(solution)/shard_map/pallas_call | solution.py:66
Async XLA Ops:
  0.0 102.0 %copy-start.4 = (s32[1,8,8]{2,1,0:T(8,128)S(1)}, s32[1,8,8]{2,1,0:T(8,128)}, u32[]{:S(2)}) copy-start(s32[1,8,8]{2,1,0:T(8,128)} %param.12) | copy-start | bytes 772
  0.0 1.4 %copy-start = (bf16[1,448,1536]{2,1,0:T(8,128)(2,1)S(1)}, bf16[1,448,1536]{2,1,0:T(8,128)(2,1)}, u32[]{:S(2)}) copy-start(bf16[1,448,1536]{2,1,0:T(8,128)(2,1)} %param.7) | copy-start | bytes 4128772
  1.4 1.2 copy-start.1
  2.5 0.7 copy-start.3
  3.2 0.7 copy-start.5
  3.9 98.2 %copy-start.2 = (f32[4608]{0:T(1024)S(1)}, f32[4608]{0:T(1024)}, u32[]{:S(2)}) copy-start(f32[4608]{0:T(1024)} %bv_ref.1) | copy-start | bytes 55300
  3.9 98.2 %copy-start.6 = (s32[1,8,8]{2,1,0:T(8,128)S(1)}, s32[1,8,8]{2,1,0:T(8,128)}, u32[]{:S(2)}) copy-start(s32[1,8,8]{2,1,0:T(8,128)} %param.13) | copy-start | bytes 772
  3.9 98.2 %copy-start.7 = (f32[1536]{0:T(1024)S(1)}, f32[1536]{0:T(1024)}, u32[]{:S(2)}) copy-start(f32[1536]{0:T(1024)} %gain_ref.1) | copy-start | bytes 18436
  3.9 98.2 %copy-start.8 = (f32[1536]{0:T(1024)S(1)}, f32[1536]{0:T(1024)}, u32[]{:S(2)}) copy-start(f32[1536]{0:T(1024)} %shift_ref.1) | copy-start | bytes 18436

commit v5 on v3

--- a/solution.py
+++ b/solution.py
@@ -207,8 +207,6 @@
             device_id_type=MESH,
         )
 
-    for j in range(1, n_dp):
-        image(j).start()
     own_image = pltpu.make_async_copy(outgoing.at[0], got_ref.at[dp], local_sem.at[0])
     own_image.start()
     own_shard = pltpu.make_async_copy(shard_ref, all_ref.at[dp, core], local_sem.at[1])
@@ -252,6 +250,9 @@
     for d in range(1, nz + 2):
         if d < nz:
             from_z(d)
+        if d == nz - 1:
+            for j in range(1, n_dp):
+                image(j).start()
         if d <= nz:
             from_x(d - 1)
         if 2 <= d <= nz:

time: 117 us -> 106 us (0.906)
  Pallas kernels: 113 us -> 102 us
    pallas_call x1, Pallas kernels: 86.6 us -> 75 us  [move_by_copies(): pl.pallas_call(functools.partial(move_kernel, n_dp, cap), in_specs=[pl.Bl...]
where the time goes in v5:
time: 106 us
  Pallas kernels  102 us (96%)
  local copies, waits for them, and re-layouts  3.91 us (4%)
    pallas_call x1, Pallas kernels, move_by_copies(): pl.pallas_call(functools.partial(move_kernel, n_dp, cap), in_specs=[pl.Bl...  75 us
    pallas_call x1, Pallas kernels, attend(): pl.pallas_call(functools.partial(attend_kernel, n_images, cap), grid=(ste...  26.5 us
    unnamed x18, local copies, waits for them, and re-layouts  3.91 us

profile of v5, /device:TPU:1, one launch (start us, length us, event | category | flops | bytes accessed | tf_op | source)
XLA Modules:
  0.0 105.5 jit_solution(9905566124838900270)
XLA Ops:
  0.0 0.0 copy-start.4
  0.0 0.0 copy-start
  0.0 1.4 %copy-done = bf16[1,448,1536]{2,1,0:T(8,128)(2,1)S(1)} copy-done((bf16[1,448,1536]{2,1,0:T(8,128)(2,1)S(1)}, bf16[1,448,1536]{2,1,0:T(8,128)(2,1)}, u32[]{:S(2)}) %copy-start) | copy-done | bytes 1376280
  1.4 0.0 copy-start.1
  1.4 1.2 %copy-done.1 = bf16[1536,288]{0,1:T(8,128)(2,1)S(1)} copy-done((bf16[1536,288]{0,1:T(8,128)(2,1)S(1)}, bf16[1536,288]{0,1:T(8,128)(2,1)}, u32[]{:S(2)}) %copy-start.1) | copy-done | bytes 884760
  2.5 0.0 copy-start.3
  2.5 0.7 copy-done.3
  3.2 0.0 copy-start.5
  3.2 0.7 copy-done.5
  3.9 0.0 copy-start.2
  3.9 0.0 copy-start.6
  3.9 0.0 copy-start.7
  3.9 0.0 copy-start.8
  3.9 75.0 %shard_map.73 = (bf16[8,56,1536]{2,1,0:T(8,128)(2,1)S(1)}, bf16[8,2,3,96,1536]{4,3,2,1,0:T(8,128)(2,1)}) custom-call(s32[8,8]{1,0:T(8,128)S(1)} %bitcast.10, s32[8,8]{1,0:T(8,128)S(1)} %bitcast.12, bf16[448,1536]{1,0:T(8,128)(2,1)S(1)} %bitcast.8, bf16[3,96,1536]{2,1,0:T(8,128)(2,1)S(1)} %bitcast.9), custom_call_target="tpu_custom_call" | custom-call | tf_op jit(solution)/shard_map/pallas_call | solution.py:282
  79.0 0.0 copy-done.4
  79.0 0.0 copy-done.2
  79.0 0.0 copy-done.6
  79.0 0.0 copy-done.7
  79.0 0.0 copy-done.8
  79.0 26.5 %shard_map.74 = bf16[8,56,1536]{2,1,0:T(8,128)(2,1)} custom-call(s32[8,8]{1,0:T(8,128)S(1)} %bitcast.11, s32[8,8]{1,0:T(8,128)S(1)} %bitcast.13, bf16[8,56,1536]{2,1,0:T(8,128)(2,1)S(1)} %get-tuple-element.7.got_ref, f32[1536]{0:T(1024)S(1)} %copy-done.7, f32[1536]{0:T(1024)S(1)} %copy-done.8, f32[4608]{0:T(1024)S(1)} %copy-done.2, f32[4608]{0:T(1024)S(1)} %copy-done.2, ...), custom_call_target="tpu_custom_call" | custom-call | flops 6341787648 | bytes 14155776 | tf_op jit(solution)/shard_map/pallas_call | solution.py:66
Async XLA Ops:
  0.0 79.0 %copy-start.4 = (s32[1,8,8]{2,1,0:T(8,128)S(1)}, s32[1,8,8]{2,1,0:T(8,128)}, u32[]{:S(2)}) copy-start(s32[1,8,8]{2,1,0:T(8,128)} %param.12) | copy-start | bytes 772
  0.0 1.4 %copy-start = (bf16[1,448,1536]{2,1,0:T(8,128)(2,1)S(1)}, bf16[1,448,1536]{2,1,0:T(8,128)(2,1)}, u32[]{:S(2)}) copy-start(bf16[1,448,1536]{2,1,0:T(8,128)(2,1)} %param.7) | copy-start | bytes 4128772
  1.4 1.2 %copy-start.1 = (bf16[1536,288]{0,1:T(8,128)(2,1)S(1)}, bf16[1536,288]{0,1:T(8,128)(2,1)}, u32[]{:S(2)}) copy-start(bf16[1536,288]{0,1:T(8,128)(2,1)} %param.10) | copy-start | bytes 2654212
  2.5 0.7 copy-start.3
  3.2 0.7 copy-start.5
  3.9 75.1 %copy-start.2 = (f32[4608]{0:T(1024)S(1)}, f32[4608]{0:T(1024)}, u32[]{:S(2)}) copy-start(f32[4608]{0:T(1024)} %bv_ref.1) | copy-start | bytes 55300
  3.9 75.1 %copy-start.6 = (s32[1,8,8]{2,1,0:T(8,128)S(1)}, s32[1,8,8]{2,1,0:T(8,128)}, u32[]{:S(2)}) copy-start(s32[1,8,8]{2,1,0:T(8,128)} %param.13) | copy-start | bytes 772
  3.9 75.1 %copy-start.7 = (f32[1536]{0:T(1024)S(1)}, f32[1536]{0:T(1024)}, u32[]{:S(2)}) copy-start(f32[1536]{0:T(1024)} %gain_ref.1) | copy-start | bytes 18436
  3.9 75.1 %copy-start.8 = (f32[1536]{0:T(1024)S(1)}, f32[1536]{0:T(1024)}, u32[]{:S(2)}) copy-start(f32[1536]{0:T(1024)} %shift_ref.1) | copy-start | bytes 18436

commit v6 on v5

--- a/solution.py
+++ b/solution.py
@@ -111,7 +111,7 @@
 PARTS = 3
 
 
-def move_kernel(n_dp, cap, len_ref, dest_ref, rows_ref, shard_ref, got_ref, all_ref, outgoing, up_sem, down_sem, x_sem, y_sem, core_sem, ring_in, core_in, image_out, image_in, local_sem):
+def move_kernel(n_dp, cap, len_ref, dest_ref, patches_ref, shard_ref, got_ref, all_ref, rows_ref, outgoing, up_sem, down_sem, x_sem, y_sem, core_sem, ring_in, core_in, image_out, image_in, local_sem):
     group, dp, core = lax.axis_index("group"), lax.axis_index("dp"), lax.axis_index("fsdp")
     nz = n_dp // 2
     z = dp // 2
@@ -121,6 +121,8 @@
     replica = (1 - group, dp, core)
     mate = (group, dp, 1 - core)
 
+    load = pltpu.make_async_copy(patches_ref, rows_ref, local_sem.at[2])
+    load.start()
     barrier = pltpu.get_barrier_semaphore()
     for j in range(1, n_dp):
         pl.semaphore_signal(barrier, inc=1, device_id=(group, (dp + j) % n_dp, core), device_id_type=MESH)
@@ -182,6 +184,7 @@
             start = start + own_len[i]
         picks.append(jnp.where((row_at < length) & (column_at == row_at + offset), 1.0, 0.0))
     pick = jnp.concatenate(picks, axis=0).astype(BF16)
+    load.wait()
     picked = jnp.dot(pick, rows_ref[...], preferred_element_type=F32)
     for j in range(n_dp):
         outgoing[j] = picked[j * cap : (j + 1) * cap].astype(BF16)
@@ -284,7 +287,7 @@
         in_specs=[
             pl.BlockSpec(memory_space=pltpu.SMEM),
             pl.BlockSpec(memory_space=pltpu.SMEM),
-            pl.BlockSpec(memory_space=pltpu.VMEM),
+            pl.BlockSpec(memory_space=pl.ANY),
             pl.BlockSpec(memory_space=pl.ANY),
         ],
         out_specs=[pl.BlockSpec(memory_space=pl.ANY)] * 2,
@@ -292,7 +295,7 @@
             jax.ShapeDtypeStruct((n_dp, cap, width), BF16),
             jax.ShapeDtypeStruct((n_dp, n_core, PARTS, columns // PARTS, width), BF16),
         ],
-        scratch_shapes=[pltpu.VMEM((n_dp, cap, width), BF16)] + [dma((n_dp, PARTS))] * 7 + [dma((n_dp,))] * 2 + [dma((2,))],
+        scratch_shapes=[pltpu.VMEM((n_dp * cap, width), BF16), pltpu.VMEM((n_dp, cap, width), BF16)] + [dma((n_dp, PARTS))] * 7 + [dma((n_dp,))] * 2 + [dma((3,))],
         compiler_params=pltpu.CompilerParams(collective_id=0, has_side_effects=True, vmem_limit_bytes=40 * 2**20),
     )(table_len, table_dest, patches, shard)
     return got, gathered.reshape(n_dp * n_core * columns, width)

time: 106 us -> 106 us (level)
  no operation moved by 1% of the time
where the time goes in v6:
time: 106 us
  Pallas kernels  102 us (96%)
  local copies, waits for them, and re-layouts  3.91 us (4%)
    pallas_call x1, Pallas kernels, move_by_copies(): pl.pallas_call(functools.partial(move_kernel, n_dp, cap), in_specs=[pl.Bl...  75.2 us
    pallas_call x1, Pallas kernels, attend(): pl.pallas_call(functools.partial(attend_kernel, n_images, cap), grid=(ste...  26.5 us
    unnamed x18, local copies, waits for them, and re-layouts  3.91 us

profile of v6, /device:TPU:1, one launch (start us, length us, event | category | flops | bytes accessed | tf_op | source)
XLA Modules:
  0.0 105.7 jit_solution(13993780902011978973)
XLA Ops:
  0.0 0.0 copy-start.4
  0.0 0.0 copy-start
  0.0 1.4 %copy-done = bf16[1,448,1536]{2,1,0:T(8,128)(2,1)S(1)} copy-done((bf16[1,448,1536]{2,1,0:T(8,128)(2,1)S(1)}, bf16[1,448,1536]{2,1,0:T(8,128)(2,1)}, u32[]{:S(2)}) %copy-start) | copy-done | bytes 1376280
  1.4 0.0 copy-start.1
  1.4 1.2 %copy-done.1 = bf16[1536,288]{0,1:T(8,128)(2,1)S(1)} copy-done((bf16[1536,288]{0,1:T(8,128)(2,1)S(1)}, bf16[1536,288]{0,1:T(8,128)(2,1)}, u32[]{:S(2)}) %copy-start.1) | copy-done | bytes 884760
  2.5 0.0 copy-start.3
  2.5 0.7 copy-done.3
  3.2 0.0 copy-start.5
  3.2 0.7 copy-done.5
  3.9 0.0 copy-start.2
  3.9 0.0 copy-start.6
  3.9 0.0 copy-start.7
  3.9 0.0 copy-start.8
  3.9 75.2 %shard_map.73 = (bf16[8,56,1536]{2,1,0:T(8,128)(2,1)S(1)}, bf16[8,2,3,96,1536]{4,3,2,1,0:T(8,128)(2,1)}) custom-call(s32[8,8]{1,0:T(8,128)S(1)} %bitcast.10, s32[8,8]{1,0:T(8,128)S(1)} %bitcast.12, bf16[448,1536]{1,0:T(8,128)(2,1)S(1)} %bitcast.8, bf16[3,96,1536]{2,1,0:T(8,128)(2,1)S(1)} %bitcast.9), custom_call_target="tpu_custom_call" | custom-call | tf_op jit(solution)/shard_map/pallas_call | solution.py:285
  79.1 0.0 copy-done.4
  79.2 0.0 copy-done.2
  79.2 0.0 copy-done.6
  79.2 0.0 copy-done.7
  79.2 0.0 copy-done.8
  79.2 26.5 %shard_map.74 = bf16[8,56,1536]{2,1,0:T(8,128)(2,1)} custom-call(s32[8,8]{1,0:T(8,128)S(1)} %bitcast.11, s32[8,8]{1,0:T(8,128)S(1)} %bitcast.13, bf16[8,56,1536]{2,1,0:T(8,128)(2,1)S(1)} %get-tuple-element.7.got_ref, f32[1536]{0:T(1024)S(1)} %copy-done.7, f32[1536]{0:T(1024)S(1)} %copy-done.8, f32[4608]{0:T(1024)S(1)} %copy-done.2, f32[4608]{0:T(1024)S(1)} %copy-done.2, ...), custom_call_target="tpu_custom_call" | custom-call | flops 6341787648 | bytes 14155776 | tf_op jit(solution)/shard_map/pallas_call | solution.py:66
Async XLA Ops:
  0.0 79.2 %copy-start.4 = (s32[1,8,8]{2,1,0:T(8,128)S(1)}, s32[1,8,8]{2,1,0:T(8,128)}, u32[]{:S(2)}) copy-start(s32[1,8,8]{2,1,0:T(8,128)} %param.12) | copy-start | bytes 772
  0.0 1.4 %copy-start = (bf16[1,448,1536]{2,1,0:T(8,128)(2,1)S(1)}, bf16[1,448,1536]{2,1,0:T(8,128)(2,1)}, u32[]{:S(2)}) copy-start(bf16[1,448,1536]{2,1,0:T(8,128)(2,1)} %param.7) | copy-start | bytes 4128772
  1.4 1.2 %copy-start.1 = (bf16[1536,288]{0,1:T(8,128)(2,1)S(1)}, bf16[1536,288]{0,1:T(8,128)(2,1)}, u32[]{:S(2)}) copy-start(bf16[1536,288]{0,1:T(8,128)(2,1)} %param.10) | copy-start | bytes 2654212
  2.5 0.7 copy-start.3
  3.2 0.7 copy-start.5
  3.9 75.3 %copy-start.2 = (f32[4608]{0:T(1024)S(1)}, f32[4608]{0:T(1024)}, u32[]{:S(2)}) copy-start(f32[4608]{0:T(1024)} %bv_ref.1) | copy-start | bytes 55300
  3.9 75.3 %copy-start.6 = (s32[1,8,8]{2,1,0:T(8,128)S(1)}, s32[1,8,8]{2,1,0:T(8,128)}, u32[]{:S(2)}) copy-start(s32[1,8,8]{2,1,0:T(8,128)} %param.13) | copy-start | bytes 772
  3.9 75.3 %copy-start.7 = (f32[1536]{0:T(1024)S(1)}, f32[1536]{0:T(1024)}, u32[]{:S(2)}) copy-start(f32[1536]{0:T(1024)} %gain_ref.1) | copy-start | bytes 18436
  3.9 75.3 %copy-start.8 = (f32[1536]{0:T(1024)S(1)}, f32[1536]{0:T(1024)}, u32[]{:S(2)}) copy-start(f32[1536]{0:T(1024)} %shift_ref.1) | copy-start | bytes 18436
